TPU v7x, 512 devices: a whole 4x4x16 slice. The times are simulated.
512 devices in a mesh: ens: 8 (over z_hi, x), node: 64 (over y, z_lo, core).
Axes of the slice: x: 4, y: 4, z: 16 (z_hi: 2, z_lo: 8; z = z_hi * 8 + z_lo), core: 2. Of those that a mesh axis runs over, the one named last changes fastest.
Arguments:
- latent: bfloat16 [8, 8192, 1024], P('ens', 'node'), may hold values from -48 to 48, as said below
- gain: float32 [1024], replicated, may hold values from 0.1 to 1.9
- w_query: bfloat16 [1024, 1024], P('node'), may hold values from -0.1875 to 0.1875
- w_key: bfloat16 [1024, 1024], P('node'), may hold values from -0.1875 to 0.1875
- w_value: bfloat16 [1024, 1024], P('node'), may hold values from -0.1875 to 0.1875
- w_read: bfloat16 [1024, 128], replicated, may hold values from -0.1875 to 0.1875
- target: float32 [8192, 128], P('node'), may hold values from -6 to 6
- neighbours: int32 [8192, 8], P('node'), may hold values from 0 to 8191, as said below
- slot_mask: int32 [8192, 8], P('node'), may hold values from 0 to 1, as said below
Outputs:
- crps: float32 [8192, 128], P('node', 'ens')
- grad_latent: float32 [8, 8192, 1024], P('ens', 'node')
Inputs may be any that keep to these rules, and one draw needn't show every extreme that they name: `latent`: positive and negative activations; the scale varies from node to node and from feature to feature. `neighbours`: slot 0 of node i holds i. Every entry lies within 64 places of its own node in the cyclic node order; some nodes reach exactly 64 on either side. Unused slots hold the node itself. `slot_mask`: slots 0 and 1 are used in every row; the used slots of a row come first.
All inputs are finite; a program needn't handle non-finite values.
Results may differ from a plain program's by a relative error of at most 0.03.
Values may be sent and summed in bfloat16 or wider, within the bound.
A program may use at most 64 MiB of HBM per device.

v0:
```python
import jax
import jax.numpy as jnp
from jax import lax
from jax.sharding import PartitionSpec as P

HEAD_DIM = 64
SLOTS = 8
HALO = 64


EPSILON = 1e-06
SOFTNESS = 0.1


def with_halo(value, sides, width):
    for axis, dim in sides:
        peers, length = (lax.axis_size(axis), value.shape[dim])
        up = [(i, (i + 1) % peers) for i in range(peers)]
        down = [(j, i) for i, j in up]
        last = lax.slice_in_dim(value, length - width, length, axis=dim)
        first = lax.slice_in_dim(value, 0, width, axis=dim)
        before = lax.ppermute(last, axis, up)
        after = lax.ppermute(first, axis, down)
        value = jnp.concatenate([before, value, after], axis=dim)
    return value


def from_behind(block, axis, distance):
    devices = range(lax.axis_size(axis))
    route = [((i - distance) % len(devices), i) for i in devices]
    return lax.ppermute(block, axis, route)


def smooth_abs(gap):
    return jnp.sqrt(gap * gap + SOFTNESS * SOFTNESS)


def smooth_sign(gap):
    return gap / jnp.sqrt(gap * gap + SOFTNESS * SOFTNESS)


def local(latent, gain, w_query, w_key, w_value, w_read, target, neighbours, slot_mask):
    rows = latent.shape[1]
    width = latent.shape[2]
    heads = width // HEAD_DIM
    parts = lax.axis_size("node")
    place = lax.axis_index("node")
    contract = (((1,), (1,)), ((), ()))
    widened = latent[0].astype(jnp.float32)
    inverse = lax.rsqrt(jnp.mean(widened * widened, axis=-1, keepdims=True) + EPSILON)
    normed = (widened * inverse * gain).astype(jnp.bfloat16)
    pieces = (
        lax.all_gather(w_query, "node", axis=0, tiled=True),
        lax.all_gather(w_key, "node", axis=0, tiled=True),
        lax.all_gather(w_value, "node", axis=0, tiled=True),
    )
    columns = normed
    projected = tuple(
        (jnp.dot(columns, piece, preferred_element_type=jnp.float32) for piece in pieces)
    )
    queries = projected[0].astype(jnp.bfloat16)
    keys = projected[1].astype(jnp.bfloat16)
    values = projected[2].astype(jnp.bfloat16)
    total_nodes = rows * parts
    own_ids = place * rows + jnp.arange(rows, dtype=jnp.int32)
    offsets = (neighbours - own_ids[:, None] + total_nodes + HALO) % total_nodes - HALO
    local_ids = jnp.arange(rows, dtype=jnp.int32)[:, None] + offsets + HALO
    valid = slot_mask > 0
    stacked = jnp.stack([keys, values])
    extended = with_halo(stacked, (("node", 1),), HALO)
    block = min(256, rows)
    blocks = rows // block
    window = block + 2 * HALO
    scale = HEAD_DIM ** (-0.5)

    def forward_block(index):
        start = index * block
        near = extended[:, local_ids]
        query_h = queries.reshape(block, heads, HEAD_DIM)
        key_h = near[0].reshape(block, SLOTS, heads, HEAD_DIM)
        value_h = near[1].reshape(block, SLOTS, heads, HEAD_DIM)
        scores = (
            jnp.einsum("bhd,bkhd->bkh", query_h, key_h, preferred_element_type=jnp.float32) * scale
        )
        weights = jnp.where(valid[:, :, None], jnp.exp(scores), 0.0)
        probs = weights / jnp.sum(weights, axis=1, keepdims=True)
        rounded = probs.astype(jnp.bfloat16)
        mixed = jnp.einsum("bkh,bkhd->bhd", rounded, value_h, preferred_element_type=jnp.float32)
        return (probs, mixed.reshape(block, width))

    probs_all, mixed = lax.map(forward_block, jnp.arange(blocks, dtype=jnp.int32))
    updated = (widened + mixed.reshape(rows, width)).astype(jnp.bfloat16)
    field = jnp.dot(updated, w_read, preferred_element_type=jnp.float32)
    members = lax.axis_size("ens")
    member = lax.axis_index("ens")
    share = field.shape[1] // members
    target_cols = lax.dynamic_slice_in_dim(target, member * share, share, 1)
    every = lax.all_gather(field[None], "ens", axis=0, tiled=True)
    columns = lax.dynamic_slice_in_dim(every, member * share, share, 2)
    gaps = columns[:, None] - columns[None]
    returned = jnp.sum(smooth_sign(field[None] - every), axis=0)
    spread = jnp.sum(smooth_abs(gaps), axis=(0, 1))
    crps = jnp.mean(smooth_abs(columns - target_cols[None]), axis=0) - spread / (
        2.0 * members * (members - 1)
    )
    pull = smooth_sign(field - target) - returned / (members - 1)
    down = lax.dot_general(
        pull.astype(jnp.bfloat16), w_read, contract, preferred_element_type=jnp.float32
    )
    down_b = down.astype(jnp.bfloat16)
    positions = jnp.arange(window, dtype=jnp.int32)

    def backward_block(carry, index):
        start = index * block
        probs = probs_all[index]
        rounded = probs.astype(jnp.bfloat16)
        near = extended[:, local_ids]
        query_h = queries.reshape(block, heads, HEAD_DIM)
        key_h = near[0].reshape(block, SLOTS, heads, HEAD_DIM)
        value_h = near[1].reshape(block, SLOTS, heads, HEAD_DIM)
        grad_h = down_b.reshape(block, heads, HEAD_DIM)
        dprob = jnp.einsum("bhd,bkhd->bkh", grad_h, value_h, preferred_element_type=jnp.float32)
        dscore = probs * (dprob - jnp.sum(probs * dprob, axis=1, keepdims=True))
        dscaled = (dscore * scale).astype(jnp.bfloat16)
        dquery = jnp.einsum("bkh,bkhd->bhd", dscaled, key_h, preferred_element_type=jnp.float32)
        relative = local_ids - start
        selector = (relative[:, :, None] == positions[None, None, :]).astype(jnp.bfloat16)
        key_coef = jnp.einsum("bkn,bkh->nbh", selector, dscaled, preferred_element_type=jnp.float32)
        value_coef = jnp.einsum(
            "bkn,bkh->nbh", selector, rounded, preferred_element_type=jnp.float32
        )
        key_part = jnp.einsum(
            "nbh,bhd->nhd", key_coef, query_h.astype(jnp.float32), precision=lax.Precision.HIGHEST
        )
        value_part = jnp.einsum(
            "nbh,bhd->nhd", value_coef, grad_h.astype(jnp.float32), precision=lax.Precision.HIGHEST
        )
        addition = jnp.stack([key_part.reshape(window, width), value_part.reshape(window, width)])
        current = carry
        carry = current + addition
        return (carry, dquery.reshape(block, width).astype(jnp.bfloat16))

    accum = jnp.zeros((2, rows + 2 * HALO, width), jnp.float32)
    accum, dquery = lax.scan(backward_block, accum, jnp.arange(blocks, dtype=jnp.int32))
    dquery = dquery.reshape(rows, width)
    lower = accum[:, :HALO]
    upper = accum[:, HALO + rows :]
    inner = accum[:, HALO : HALO + rows]
    from_next = from_behind(lower.astype(jnp.bfloat16), "node", -1).astype(lower.dtype)
    from_prev = from_behind(upper.astype(jnp.bfloat16), "node", 1).astype(upper.dtype)
    inner = inner.at[:, rows - HALO :].add(from_next)
    inner = inner.at[:, :HALO].add(from_prev)
    key_grad = inner[0].astype(jnp.bfloat16)
    value_grad = inner[1].astype(jnp.bfloat16)
    grads_in = (dquery, key_grad, value_grad)
    pieces = (
        lax.all_gather(w_query, "node", axis=0, tiled=True),
        lax.all_gather(w_key, "node", axis=0, tiled=True),
        lax.all_gather(w_value, "node", axis=0, tiled=True),
    )
    term = lax.dot_general(grads_in[0], pieces[0], contract, preferred_element_type=jnp.float32)
    term = term + lax.dot_general(
        grads_in[1], pieces[1], contract, preferred_element_type=jnp.float32
    )
    term = term + lax.dot_general(
        grads_in[2], pieces[2], contract, preferred_element_type=jnp.float32
    )
    scaled = term * gain
    norm_back = inverse * scaled - widened * inverse * inverse * inverse * jnp.mean(
        scaled * widened, axis=-1, keepdims=True
    )
    grad_latent = (down + norm_back)[None]
    return (crps, grad_latent)


def solution(mesh):
    placed = (
        P("ens", "node", None),
        P(),
        P("node", None),
        P("node", None),
        P("node", None),
        P(),
        P("node", None),
        P("node", None),
        P("node", None),
    )
    return jax.shard_map(
        local,
        mesh=mesh,
        in_specs=placed,
        out_specs=(P("node", "ens"), P("ens", "node", None)),
        check_vma=False,
    )
```

profile of v0, /device:TPU:1, one launch (start us, length us, event | category | flops | bytes accessed | tf_op | source)
XLA Modules:
  0.0 543.9 jit_solution(868424001686496909)
XLA Ops:
  14.0 122.7 %all-gather.5.cloned.1.call-done = bf16[1024,1024]{1,0:T(8,128)(2,1)} async-done(((bf16[16,1024]{1,0:T(8,128)(2,1)}), bf16[1024,1024]{1,0:T(8,128)(2,1)}) %all-gather.5.cloned.1.call-update) | async-done | bytes 2097168 | tf_op jit(solution)/shard_map/all_gather | solution.py:54
  136.7 2.2 fusion.11
  138.9 116.5 %all-gather.7.cloned.1.call-done = bf16[1024,1024]{1,0:T(8,128)(2,1)} async-done(((bf16[16,1024]{1,0:T(8,128)(2,1)}), bf16[1024,1024]{1,0:T(8,128)(2,1)}) %all-gather.7.cloned.1.call-update) | async-done | bytes 2097168 | tf_op jit(solution)/shard_map/all_gather | solution.py:55
  255.4 2.1 fusion.12
  257.5 2.2 collective-permute-start.1
  259.7 3.4 collective-permute-start
  263.1 110.9 %all-gather.9.cloned.1.call-done = bf16[1024,1024]{1,0:T(8,128)(2,1)} async-done(((bf16[16,1024]{1,0:T(8,128)(2,1)}), bf16[1024,1024]{1,0:T(8,128)(2,1)}) %all-gather.9.cloned.1.call-update) | async-done | bytes 2097168 | tf_op jit(solution)/shard_map/all_gather | solution.py:53
  374.0 2.1 convolution_convert_fusion
  379.3 15.6 %gather_fusion = bf16[1024,2,1024]{2,1,0:T(2,128)(2,1)} fusion(bf16[2,256,1024]{2,0,1:T(2,128)(2,1)S(1)} %copy.65, s32[1024]{0:T(1024)S(1)} %broadcast_clamp_fusion), kind=kCustom, calls=%fused_computation | custom fusion | bytes 8392704 | tf_op jit(solution)/shard_map/while/body/eval_jaxpr/gather | solution.py:78
  394.9 11.2 %copy.66 = bf16[128,8,2,1024]{0,3,1,2:T(8,128)(2,1)} copy(bf16[128,8,2,1024]{3,2,1,0:T(2,128)(2,1)} %bitcast.109) | data formatting | bytes 8388608 | tf_op jit(solution)/shard_map/while/body/eval_jaxpr/gather | solution.py:78
  406.1 4.0 fusion.46
  412.3 1.2 copy.108
  413.5 3.0 multiply_reduce_fusion.2
  416.5 2.1 copy.68
  418.6 1.3 fusion.31
  419.9 58.5 %all-gather = f32[1024,128]{1,0:T(8,128)S(1)} all-gather(f32[128,128]{1,0:T(8,128)S(1)} %fusion.31), channel_id=2, replica_groups=mesh['ens'=8,'node'=64] {'ens'}, dimensions={0}, use_global_device_ids=true | all-gather | bytes 589824 | tf_op jit(solution)/shard_map/all_gather | solution.py:98
  480.8 2.4 multiply_reduce_fusion.1
  484.2 2.5 bitcast_convert_fusion
  486.6 1.3 convolution_bitcast_fusion
  488.6 2.1 fusion.4
  490.7 2.1 fusion.2
  492.8 1.4 fusion.13
  496.8 1.2 copy.110
  498.0 2.4 fusion.47
  500.3 7.8 %collective-permute-start.2 = (bf16[2,64,1024]{1,2,0:T(8,128)(2,1)S(1)}, bf16[2,64,1024]{1,2,0:T(8,128)(2,1)S(1)}, u32[]{:S(2)}, u32[]{:S(2)}) collective-permute-start(bf16[2,64,1024]{1,2,0:T(8,128)(2,1)S(1)} %get-tuple-element.81), channel_id=1, source_target_pairs={{1,0},{2,1},{3,2},{4,3},{5,4},{6,5},{7,6},{8,7},{9,8},{10,9},{11,1... | collective-permute-start | bytes 786440 | tf_op jit(solution)/shard_map/ppermute | solution.py:31
  508.2 3.9 collective-permute-start.3
  513.3 1.6 fusion.49
  514.9 1.9 collective-permute-done.2
  516.9 6.2 %scatter-add.6 = f32[2,128,1024]{1,2,0:T(8,128)S(1)} dynamic-update-slice(f32[2,128,1024]{1,2,0:T(8,128)S(1)} %copy-done.5, f32[2,64,1024]{1,2,0:T(8,128)S(1)} %fusion.15, s32[]{:T(128)} %constant.134.clone.1, s32[]{:T(128)} %constant.144.clone.1, s32[]{:T(128)} %constant.134.clone.1) | dynamic-update-slice | bytes 1048580 | tf_op jit(solution)/shard_map/scatter-add | solution.py:151
  523.1 2.1 slice_add_fusion
  525.2 7.9 %scatter-add.9 = f32[2,128,1024]{1,2,0:T(8,128)S(1)} dynamic-update-slice(f32[2,128,1024]{1,2,0:T(8,128)S(1)} %scatter-add.6, f32[2,64,1024]{1,2,0:T(8,128)} %slice_add_fusion, s32[]{:T(128)} %constant.134.clone.1, s32[]{:T(128)} %constant.134.clone.1, s32[]{:T(128)} %constant.134.clone.1) | dynamic-update-slice | bytes 1048580 | tf_op jit(solution)/shard_map/scatter-add | solution.py:152
  533.3 2.0 convolution_add_fusion.1
  (90 shorter events, 22.1 us)
Async XLA Ops:
  7.2 411.4 %copy-start = (bf16[1024,128]{1,0:T(8,128)(2,1)S(1)}, bf16[1024,128]{1,0:T(8,128)(2,1)}, u32[]{:S(2)}) copy-start(bf16[1024,128]{1,0:T(8,128)(2,1)} %param.18) | copy-start | bytes 786436
  7.2 248.2 %copy-start.3 = (bf16[1,128,1024]{2,1,0:T(8,128)(2,1)S(1)}, bf16[1,128,1024]{2,1,0:T(8,128)(2,1)}, u32[]{:S(2)}) copy-start(bf16[1,128,1024]{2,1,0:T(8,128)(2,1)} %param.13) | copy-start | bytes 786436
  7.2 248.2 %copy-start.16 = (f32[1024]{0:T(1024)S(1)}, f32[1024]{0:T(1024)}, u32[]{:S(2)}) copy-start(f32[1024]{0:T(1024)} %param.14) | copy-start | bytes 12292
  7.2 129.4 %all-gather.5.cloned.1.call-start = ((), (), s32[]{:S(2)}) async-start(), calls=%async_computation | async-start | bytes 2129920 | tf_op jit(solution)/shard_map/all_gather | solution.py:54
  7.9 247.4 %all-gather.7.cloned.1.call-start = ((), (), s32[]{:S(2)}) async-start(), calls=%async_computation.1 | async-start | bytes 2129920 | tf_op jit(solution)/shard_map/all_gather | solution.py:55
  8.7 365.3 %all-gather.9.cloned.1.call-start = ((), (), s32[]{:S(2)}) async-start(), calls=%async_computation.2 | async-start | bytes 2129920 | tf_op jit(solution)/shard_map/all_gather | solution.py:53
  14.0 360.1 %copy-start.19 = (f32[128]{0:T(128)}, f32[128]{0:T(128)S(1)}, u32[]{:S(2)}) copy-start(f32[128]{0:T(128)S(1)} %add_rsqrt_fusion) | copy-start | bytes 1540
  257.5 119.7 %collective-permute-start.1 = (bf16[2,64,1024]{2,1,0:T(8,128)(2,1)S(1)}, bf16[2,64,1024]{2,1,0:T(8,128)(2,1)S(1)}, u32[]{:S(2)}, u32[]{:S(2)}) collective-permute-start(bf16[2,64,1024]{2,1,0:T(8,128)(2,1)S(1)} %get-tuple-element.83), channel_id=1, source_target_pairs={{1,0},{2,1},{3,2},{4,3},{5,4},{6,5},{7,6},{8,7},{9,8},{10,9},{11,1... | collective-permute-start | bytes 786440 | tf_op jit(solution)/shard_map/ppermute | solution.py:23
  259.7 117.5 %collective-permute-start = (bf16[2,64,1024]{2,1,0:T(8,128)(2,1)S(1)}, bf16[2,64,1024]{2,1,0:T(8,128)(2,1)}, u32[]{:S(2)}, u32[]{:S(2)}) collective-permute-start(bf16[2,64,1024]{2,1,0:T(8,128)(2,1)S(1)} %get-tuple-element.82), channel_id=1, source_target_pairs={{0,1},{1,2},{2,3},{3,4},{4,5},{5,6},{6,7},{7,8},{8,9},{9,10},{10,1... | collective-permute-start | bytes 786440 | tf_op jit(solution)/shard_map/ppermute | solution.py:22
  376.3 3.0 copy-start.9
  406.1 4.0 copy-start.14
  418.6 60.9 %copy-start.15 = (f32[128,128]{1,0:T(8,128)S(1)}, f32[128,128]{1,0:T(8,128)}, u32[]{:S(2)}) copy-start(f32[128,128]{1,0:T(8,128)} %param.19) | copy-start | bytes 196612
  480.7 5.9 %copy-start.11 = (bf16[128,1024]{0,1:T(8,128)(2,1)}, bf16[128,1024]{0,1:T(8,128)(2,1)S(1)}, u32[]{:S(2)}) copy-start(bf16[128,1024]{0,1:T(8,128)(2,1)S(1)} %copy.73) | copy-start | bytes 786436
  486.6 2.0 copy-start.10
  488.6 2.1 copy-start.12
  492.8 1.4 copy-start.1
  494.2 2.6 copy-start.18
  498.0 15.3 %copy-start.8 = (bf16[1024,1024]{1,0:T(8,128)(2,1)S(1)}, bf16[1024,1024]{1,0:T(8,128)(2,1)}, u32[]{:S(2)}) copy-start(bf16[1024,1024]{1,0:T(8,128)(2,1)} %all-gather.9.cloned.1.call-done) | copy-start | bytes 6291460
  500.3 16.5 %collective-permute-start.2 = (bf16[2,64,1024]{1,2,0:T(8,128)(2,1)S(1)}, bf16[2,64,1024]{1,2,0:T(8,128)(2,1)S(1)}, u32[]{:S(2)}, u32[]{:S(2)}) collective-permute-start(bf16[2,64,1024]{1,2,0:T(8,128)(2,1)S(1)} %get-tuple-element.81), channel_id=1, source_target_pairs={{1,0},{2,1},{3,2},{4,3},{5,4},{6,5},{7,6},{8,7},{9,8},{10,9},{11,1... | collective-permute-start | bytes 786440 | tf_op jit(solution)/shard_map/ppermute | solution.py:31
  508.2 15.0 %collective-permute-start.3 = (bf16[2,64,1024]{1,2,0:T(8,128)(2,1)}, bf16[2,64,1024]{1,2,0:T(8,128)(2,1)}, u32[]{:S(2)}, u32[]{:S(2)}) collective-permute-start(bf16[2,64,1024]{1,2,0:T(8,128)(2,1)} %get-tuple-element.80), channel_id=1, source_target_pairs={{63,0},{0,1},{1,2},{2,3},{3,4},{4,5},{5,6},{6,7},{7,8},{8,9},{9,10... | collective-permute-start | bytes 786440 | tf_op jit(solution)/shard_map/ppermute | solution.py:31
  512.7 4.1 copy-start.2
  514.9 2.1 copy-start.5
  525.2 8.0 %copy-start.6 = (bf16[1024,1024]{1,0:T(8,128)(2,1)S(1)}, bf16[1024,1024]{1,0:T(8,128)(2,1)}, u32[]{:S(2)}) copy-start(bf16[1024,1024]{1,0:T(8,128)(2,1)} %all-gather.5.cloned.1.call-done) | copy-start | bytes 6291460
  533.2 2.1 copy-start.4
  533.2 2.1 copy-start.7
  533.3 2.1 copy-start.17
  535.3 1.0 copy-start.13
  535.3 1.0 copy-start.20
Sparse Core Ops, SparseCore 0:
  10.2 126.4 all-gather.4
  138.8 116.4 all-gather.6
  257.5 116.4 all-gather.8
where the time goes:
time: 550 us; the launch traced here: 544 us
  waiting for transfers between devices  354 us (64%)
  local copies, waits for them, and re-layouts  58.7 us (11%)
  blocking collectives  58.5 us (11%)
  other arithmetic  21.6 us (4%)
  matrix products  19.4 us (4%)
  starting transfers between devices  17.4 us (3%)
  between operations  14.2 us (3%)
    all_gather x1, waiting for transfers between devices, local(): lax.all_gather(w_key, 'node', axis=0, tiled=True)  123 us
    all_gather x1, waiting for transfers between devices, local(): lax.all_gather(w_value, 'node', axis=0, tiled=True)  116 us
    all_gather x1, waiting for transfers between devices, local(): lax.all_gather(w_query, 'node', axis=0, tiled=True)  111 us
    all_gather x1, blocking collectives, local(): every = lax.all_gather(field[None], 'ens', axis=0, tiled=True)  58.5 us
    gather x2, local copies, waits for them, and re-layouts, forward_block(): near = extended[:, local_ids]  26.8 us
    ppermute x2, starting transfers between devices, from_behind(): return lax.ppermute(block, axis, route)  11.7 us
  transfers between devices with their start and end apart: 7, of which 4 were waited for; matrix products, arithmetic and copies ran while one was open for 4% of the time, Pallas kernels for 0%

commit v1 on v0

v1 whole, which is shorter than its diff:
```python
import jax
import jax.numpy as jnp
from jax import lax
from jax.experimental import pallas as pl
from jax.experimental.pallas import tpu as pltpu
from jax.sharding import PartitionSpec as P

HEAD_DIM = 64
SLOTS = 8
HALO = 64
EPSILON = 1e-06
SOFTNESS = 0.1

D = 1024
V = 128
ROWS = 128
PAIR = 2 * ROWS
NEAR = PAIR + 2 * HALO
HALF = D // 2
WINDOW = ROWS + 2 * HALO
GROUPS = HALF // 128
MEMBERS = 8
X, Y, Z, Z_LO = 4, 4, 16, 8
CHIPS = Y * Z_LO
MESH = pl.DeviceIdType.MESH
COPIES = 160

F32 = jnp.float32
BF16 = jnp.bfloat16
NT = (((1,), (1,)), ((), ()))
TN = (((0,), (0,)), ((), ()))


def dot(a, b):
    return jnp.dot(a, b, preferred_element_type=F32)


def dot_nt(a, b):
    return lax.dot_general(a, b, NT, preferred_element_type=F32)


def dot_tn(a, b):
    return lax.dot_general(a, b, TN, preferred_element_type=F32)


class Place:
    def __init__(self):
        self.member = lax.axis_index("ens")
        self.node = lax.axis_index("node")
        self.x = self.member % X
        self.y = self.node // (2 * Z_LO)
        self.z = (self.member // X) * Z_LO + (self.node // 2) % Z_LO
        self.core = self.node % 2

    def at(self, dx=0, dy=0, dz=0, dc=0):
        x, y, z = (self.x + dx + X) % X, (self.y + dy + Y) % Y, (self.z + dz + Z) % Z
        core = (self.core + dc) % 2
        return {"ens": (z // Z_LO) * X + x, "node": (y * Z_LO + z % Z_LO) * 2 + core}

    def chip(self, step, core):
        return {"ens": self.member, "node": ((self.node // 2 + step + CHIPS) % CHIPS) * 2 + core}


class Net:
    def __init__(self, send_sem, recv_sem):
        self.send_sem, self.recv_sem = send_sem, recv_sem
        self.count = 0
        self.sent = []

    def send(self, src, dst, to):
        copy = pltpu.make_async_remote_copy(
            src_ref=src,
            dst_ref=dst,
            send_sem=self.send_sem.at[self.count],
            recv_sem=self.recv_sem.at[self.count],
            device_id=to,
            device_id_type=MESH,
        )
        self.count += 1
        copy.start()
        self.sent.append(copy)
        return copy

    def drain(self):
        for copy in self.sent:
            copy.wait_send()


def gather_weights(here, net, w_refs, W, local_sem):
    y, z, c = here.y, here.z % Z_LO, here.core
    mine, other = pl.multiple_of(c * HALF, HALF), pl.multiple_of((1 - c) * HALF, HALF)
    own_rows = pl.ds(pl.multiple_of(c * 16, 16), 16)
    local, swap = [], []
    for i, w in enumerate(w_refs):
        spot = W.at[i, y, z, own_rows]
        swap.append(net.send(w.at[:, pl.ds(other, HALF)], spot, here.at(dc=1)))
        local.append(pltpu.make_async_copy(w.at[:, pl.ds(mine, HALF)], spot, local_sem.at[i]))
        local[-1].start()
    for copy in local:
        copy.wait()
    for copy in swap:
        copy.wait_recv()

    first, second = pl.ds(0, 16), pl.ds(16, 16)
    kept = pl.ds(here.x % 2, 2)
    given = (here.x % 2) * 2
    across = []

    def pass_on(rows, ys, zs):
        piece = W.at[given, ys, zs, rows]
        across.append(net.send(piece, piece, here.at(dx=1 if rows is first else -1)))

    def forward(ys, zs, rows, **step):
        piece = W.at[kept, ys, zs, rows]
        return net.send(piece, piece, here.at(**step))

    every = slice(None)
    below, above, far = (y + 3) % Y, (y + 1) % Y, (y + 2) % Y
    along_y = [forward(y, z, first, dy=d) for d in (1, -1, 2)]
    second_up, second_down = forward(y, z, second, dz=1), forward(y, z, second, dz=-1)
    pending = [(z, forward(y, z, second, dy=1), forward(y, z, second, dy=-1))]
    for copy in along_y:
        copy.wait_recv()
    first_up, first_down = forward(every, z, first, dz=1), forward(every, z, first, dz=-1)
    for ys in (below, above, far):
        pass_on(first, ys, z)
    relayed = []

    def spread(zs, from_below, from_above):
        from_below.wait_recv()
        from_above.wait_recv()
        if len(relayed) % 2 == 0:
            relayed.append((zs, forward(below, zs, second, dy=1)))
        else:
            relayed.append((zs, forward(above, zs, second, dy=-1)))
        for ys in (below, above) if zs is z else (below, above, y):
            pass_on(second, ys, zs)

    last = Z_LO // 2
    for step in range(1, last + 1):
        before, after = (z + Z_LO - step) % Z_LO, (z + step) % Z_LO
        arrived = []
        if step < last:
            second_up.wait_recv()
            if step < last - 1:
                second_up = forward(y, before, second, dz=1)
            arrived.append((before, forward(y, before, second, dy=1), forward(y, before, second, dy=-1)))
        second_down.wait_recv()
        if step < last:
            second_down = forward(y, after, second, dz=-1)
        arrived.append((after, forward(y, after, second, dy=1), forward(y, after, second, dy=-1)))
        first_up.wait_recv()
        first_down.wait_recv()
        if step < last - 1:
            first_up, first_down = forward(every, before, first, dz=1), forward(every, after, first, dz=-1)
        elif step == last - 1:
            first_up = forward(pl.ds(0, 2), before, first, dz=1)
            first_down = forward(pl.ds(2, 2), after, first, dz=-1)
        if step < last:
            pass_on(first, every, before)
        pass_on(first, every, after)
        for item in pending:
            spread(*item)
        pending = arrived
    for item in pending:
        spread(*item)
    for zs, copy in relayed:
        copy.wait_recv()
        pass_on(second, far, zs)
    for copy in across:
        copy.wait_recv()


def body(
    latent, gain, w_query, w_key, w_value, w_read, target, neighbours, slot_mask,
    crps_out, grad_out,
    W, near, normed, inverse, counts, queries, keys, values, probs, mixed,
    part, part_in, field, pull, down, dquery, dkey, dvalue, halo_out, halo_in, back, back_in,
    send_sem, recv_sem, local_sem,
):
    here = Place()
    net = Net(send_sem, recv_sem)
    core = here.core
    peers = [
        here.at(dc=1),
        here.at(dy=1), here.at(dy=-1), here.at(dy=2),
        here.at(dz=1), here.at(dz=-1), here.at(dz=8),
        here.at(dx=1), here.at(dx=-1), here.at(dx=2),
        here.chip(1, core), here.chip(-1, core), here.chip(2 * core - 1, 1 - core),
    ]
    barrier = pltpu.get_barrier_semaphore()
    for peer in peers:
        pl.semaphore_signal(barrier, inc=1, device_id=peer, device_id_type=MESH)
    pl.semaphore_wait(barrier, len(peers))

    own = pl.ds(pl.multiple_of(HALO + core * ROWS, 64), ROWS)
    edge = pl.ds(pl.multiple_of(core * HALO, 64), HALO)
    edge_there = pl.ds(pl.multiple_of((1 - core) * (HALO + PAIR), 64), HALO)
    edge_here = pl.ds(pl.multiple_of(core * (HALO + PAIR), 64), HALO)
    own_copy = pltpu.make_async_copy(latent, near.at[own], local_sem.at[3])
    own_copy.start()
    pair_copy = net.send(latent, near.at[own], here.at(dc=1))
    edge_copy = net.send(latent.at[edge], near.at[edge_there], here.chip(2 * core - 1, 1 - core))

    first = here.node * ROWS - HALO
    total = 2 * CHIPS * ROWS
    spot = neighbours[...] - first
    spot = jnp.where(spot < 0, spot + total, spot)
    spot = jnp.where(spot >= total, spot - total, spot)
    used = (slot_mask[...] > 0).astype(F32)
    window = lax.broadcasted_iota(jnp.int32, (ROWS, WINDOW), 1)
    number = jnp.zeros((ROWS, WINDOW), F32)
    for j in range(SLOTS):
        number += jnp.where(spot[:, j : j + 1] == window, used[:, j : j + 1], 0.0)
    counts[core] = number.astype(BF16)
    count_copy = net.send(counts.at[core], counts.at[core], here.at(dc=1))

    gather_weights(here, net, (w_query, w_key, w_value), W, local_sem)

    edge_copy.wait_recv()
    hand_on = net.send(near.at[edge_here], near.at[edge_here], here.at(dc=1))
    own_copy.wait()
    pair_copy.wait_recv()
    hand_on.wait_recv()
    count_copy.wait_recv()

    @pl.loop(0, NEAR // 64)
    def _(i):
        rows = pl.ds(pl.multiple_of(i * 64, 64), 64)
        wide = near[rows, :].astype(F32)
        scale = lax.rsqrt(jnp.mean(wide * wide, axis=-1, keepdims=True) + EPSILON)
        inverse[rows, :] = jnp.broadcast_to(scale, (64, 128))
        normed[rows, :] = (wide * scale * gain[...]).astype(BF16)

    inner = pl.ds(HALO, PAIR)

    @pl.loop(0, HALF // 256)
    def _(j):
        cols = pl.ds(pl.multiple_of(j * 256, 256), 256)
        queries[:, cols] = dot(normed[inner, :], W[0, :, :, :, cols].reshape(D, 256)).astype(BF16)
        keys[:, cols] = dot(normed[...], W[1, :, :, :, cols].reshape(D, 256)).astype(BF16)
        values[:, cols] = dot(normed[...], W[2, :, :, :, cols].reshape(D, 256)).astype(BF16)

    lanes = lax.broadcasted_iota(jnp.int32, (1, 128), 1)
    low = (lanes < HEAD_DIM).astype(F32)
    low_b, high_b = low.astype(BF16), (1.0 - low).astype(BF16)
    scale = HEAD_DIM ** (-0.5)

    def two_heads(piece):
        return jnp.concatenate([piece * low_b, piece * high_b], axis=0)

    def one_piece(both):
        return jnp.where(lanes < HEAD_DIM, both[:ROWS], both[ROWS:])

    def places(i):
        block, group = i // GROUPS, i % GROUPS
        rows = pl.ds(pl.multiple_of(block * ROWS, ROWS), ROWS)
        around = pl.ds(pl.multiple_of(block * ROWS, ROWS), WINDOW)
        return block, rows, around, pl.ds(pl.multiple_of(group * 128, 128), 128)

    def count_of(block):
        one = counts[block].astype(F32)
        return jnp.concatenate([one, one], axis=0)

    @pl.loop(0, 2 * GROUPS)
    def _(i):
        block, rows, around, cols = places(i)
        number = count_of(block)
        scores = dot_nt(two_heads(queries[rows, cols]), keys[around, cols])
        weight = jnp.where(number > 0, jnp.exp(scores * scale), 0.0)
        prob = weight / jnp.sum(number * weight, axis=-1, keepdims=True)
        probs[i] = prob
        share = (prob.astype(BF16).astype(F32) * number).astype(BF16)
        mixed[rows, cols] = one_piece(dot(share, values[around, cols]))

    mine = pl.ds(pl.multiple_of(core * HALF, HALF), HALF)
    updated = (near[inner, mine].astype(F32) + mixed[...]).astype(BF16)
    reader = w_read[mine, :]
    part[...] = dot(updated, reader)
    mine_rows = pl.ds(pl.multiple_of(core * ROWS, ROWS), ROWS)
    other_rows = pl.ds(pl.multiple_of((1 - core) * ROWS, ROWS), ROWS)
    part_copy = net.send(part.at[other_rows], part_in, here.at(dc=1))
    part_copy.wait_recv()
    me = here.member
    field[me] = part[mine_rows, :] + part_in[...]

    partner = (me + X) % MEMBERS
    along = [net.send(field.at[me], field.at[me], here.at(dx=d)) for d in (1, -1, 2)]
    pieces = [pl.ds(k * 32, 32) for k in range(4)]
    over = [net.send(field.at[me, rows], field.at[me, rows], here.at(dz=8)) for rows in pieces]
    for copy, rows in zip(over, pieces):
        copy.wait_recv()
        piece = field.at[partner, rows]
        along += [net.send(piece, piece, here.at(dx=d)) for d in (1, -1, 2)]
    for copy in along:
        copy.wait_recv()

    soft = SOFTNESS * SOFTNESS
    here_field = field[me]

    def sign_of(gap):
        return gap * lax.rsqrt(gap * gap + soft)

    returned = sign_of(here_field - field[0])
    for m in range(1, MEMBERS):
        returned += sign_of(here_field - field[m])
    pulled = sign_of(here_field - target[...]) - returned / (MEMBERS - 1)
    pull[core] = pulled.astype(BF16)
    pull_copy = net.send(pull.at[core], pull.at[core], here.at(dc=1))
    pull_copy.wait_recv()
    down[...] = dot_nt(pull[...].reshape(PAIR, V), reader).astype(BF16)

    dkey[...] = jnp.zeros_like(dkey)
    dvalue[...] = jnp.zeros_like(dvalue)

    def backward(i, carry):
        block, rows, around, cols = places(i)
        number = count_of(block)
        prob = probs[i]
        given = two_heads(down[rows, cols])
        asked = two_heads(queries[rows, cols])
        share = (prob.astype(BF16).astype(F32) * number).astype(BF16)
        dprob = dot_nt(given, values[around, cols])
        level = jnp.sum(number * prob * dprob, axis=-1, keepdims=True)
        dscaled = (prob * (dprob - level) * scale).astype(BF16)
        dscaled = (dscaled.astype(F32) * number).astype(BF16)
        dquery[rows, cols] = one_piece(dot(dscaled, keys[around, cols])).astype(BF16)
        dkey[around, cols] += dot_tn(dscaled, asked)
        dvalue[around, cols] += dot_tn(share, given)
        return carry

    def send_halo(side, rows, step):
        halo_out[side, 0] = dkey[rows, :].astype(BF16)
        halo_out[side, 1] = dvalue[rows, :].astype(BF16)
        return net.send(halo_out.at[side], halo_in.at[side], here.chip(step, core))

    lax.fori_loop(0, GROUPS, backward, 0)
    to_prev = send_halo(0, pl.ds(0, HALO), -1)
    lax.fori_loop(GROUPS, 2 * GROUPS, backward, 0)
    to_next = send_halo(1, pl.ds(HALO + PAIR, HALO), 1)

    @pl.loop(0, D // 256)
    def _(j):
        cols = pl.ds(pl.multiple_of(j * 256, 256), 256)
        piece = W[0, j].reshape(256, HALF)
        back[:, cols] = dot_nt(dquery[...], piece)

    to_prev.wait_recv()
    to_next.wait_recv()
    for grad, k in ((dkey, 0), (dvalue, 1)):
        grad[pl.ds(PAIR, HALO), :] += halo_in[0, k].astype(F32)
        grad[pl.ds(HALO, HALO), :] += halo_in[1, k].astype(F32)

    @pl.loop(0, D // 256)
    def _(j):
        cols = pl.ds(pl.multiple_of(j * 256, 256), 256)
        back[:, cols] += dot_nt(dkey[inner, :].astype(BF16), W[1, j].reshape(256, HALF)) + dot_nt(
            dvalue[inner, :].astype(BF16), W[2, j].reshape(256, HALF)
        )

    back_copy = net.send(back.at[other_rows], back_in, here.at(dc=1))

    def abs_of(gap):
        return jnp.sqrt(gap * gap + soft)

    spread = jnp.full((ROWS, V), MEMBERS * SOFTNESS, F32)
    miss = jnp.zeros((ROWS, V), F32)
    for m in range(MEMBERS):
        miss += abs_of(field[m] - target[...])
        for k in range(m):
            spread += 2.0 * abs_of(field[m] - field[k])
    crps = miss / MEMBERS - spread / (2.0 * MEMBERS * (MEMBERS - 1))
    share = V // MEMBERS
    crps_out[...] = pltpu.roll(crps, (V - me * share) % V, 1)[:, :share]

    back_copy.wait_recv()

    @pl.loop(0, ROWS // 32)
    def _(i):
        rows = pl.ds(pl.multiple_of(i * 32, 32), 32)
        wide = latent[rows, :].astype(F32)
        here_rows = pl.ds(pl.multiple_of(HALO + core * ROWS + i * 32, 32), 32)
        factor = inverse[here_rows, 0:1]
        pair_rows = pl.ds(pl.multiple_of(core * ROWS + i * 32, 32), 32)
        scaled = (back[pair_rows, :] + back_in[rows, :]) * gain[...]
        fall = dot_nt(pull[core, rows, :], w_read[...])
        middle = jnp.mean(scaled * wide, axis=-1, keepdims=True)
        grad_out[rows, :] = fall + factor * scaled - wide * (factor * factor * factor * middle)

    net.drain()


def local(latent, gain, w_query, w_key, w_value, w_read, target, neighbours, slot_mask):
    vmem = pl.BlockSpec(memory_space=pltpu.VMEM)
    crps, grad = pl.pallas_call(
        body,
        out_shape=(jax.ShapeDtypeStruct((ROWS, V // MEMBERS), F32), jax.ShapeDtypeStruct((ROWS, D), F32)),
        in_specs=[vmem] * 9,
        out_specs=(vmem, vmem),
        scratch_shapes=[
            pltpu.VMEM((3, Y, Z_LO, 32, HALF), BF16),
            pltpu.VMEM((NEAR, D), BF16),
            pltpu.VMEM((NEAR, D), BF16),
            pltpu.VMEM((NEAR, 128), F32),
            pltpu.VMEM((2, ROWS, WINDOW), BF16),
            pltpu.VMEM((PAIR, HALF), BF16),
            pltpu.VMEM((NEAR, HALF), BF16),
            pltpu.VMEM((NEAR, HALF), BF16),
            pltpu.VMEM((2 * GROUPS, 2 * ROWS, WINDOW), F32),
            pltpu.VMEM((PAIR, HALF), F32),
            pltpu.VMEM((PAIR, V), F32),
            pltpu.VMEM((ROWS, V), F32),
            pltpu.VMEM((MEMBERS, ROWS, V), F32),
            pltpu.VMEM((2, ROWS, V), BF16),
            pltpu.VMEM((PAIR, HALF), BF16),
            pltpu.VMEM((PAIR, HALF), BF16),
            pltpu.VMEM((NEAR, HALF), F32),
            pltpu.VMEM((NEAR, HALF), F32),
            pltpu.VMEM((2, 2, HALO, HALF), BF16),
            pltpu.VMEM((2, 2, HALO, HALF), BF16),
            pltpu.VMEM((PAIR, D), F32),
            pltpu.VMEM((ROWS, D), F32),
            pltpu.SemaphoreType.DMA((COPIES,)),
            pltpu.SemaphoreType.DMA((COPIES,)),
            pltpu.SemaphoreType.DMA((4,)),
        ],
        compiler_params=pltpu.CompilerParams(
            collective_id=0, has_side_effects=True, vmem_limit_bytes=40 * 1024 * 1024
        ),
    )(latent[0], gain[None], w_query, w_key, w_value, w_read, target, neighbours, slot_mask)
    return crps, grad[None]


def solution(mesh):
    placed = (
        P("ens", "node", None),
        P(),
        P("node", None),
        P("node", None),
        P("node", None),
        P(),
        P("node", None),
        P("node", None),
        P("node", None),
    )
    return jax.shard_map(
        local,
        mesh=mesh,
        in_specs=placed,
        out_specs=(P("node", "ens"), P("ens", "node", None)),
        check_vma=False,
    )
```

time: 550 us -> 101 us (0.18); the launches traced: 544 us -> 101 us
  waiting for transfers between devices: 354 us -> 0 us
  Pallas kernels: 0 us -> 94.5 us
  blocking collectives: 58.5 us -> 0 us
  local copies, waits for them, and re-layouts: 58.7 us -> 5.7 us
  other arithmetic: 21.6 us -> 0 us
  matrix products: 19.4 us -> 0 us
  starting transfers between devices: 17.4 us -> 0 us
  between operations: 14.2 us -> 0.69 us
    all_gather x3 -> x0, waiting for transfers between devices: 350 us -> none  [the longest x1 123 us: local(): lax.all_gather(w_key, 'node', axis=0, tiled=True)]
    pallas_call x0 -> x1, Pallas kernels: none -> 94.5 us  [local(): pl.pallas_call(body, out_shape=(jax.ShapeDtypeStruct((ROWS, V // MEMBERS)...]
    all_gather x1 -> x0, blocking collectives: 58.5 us -> none  [local(): every = lax.all_gather(field[None], 'ens', axis=0, tiled=True)]
    gather x2 -> x0, local copies, waits for them, and re-layouts: 26.8 us -> none  [forward_block(): near = extended[:, local_ids]]
    dot_general x12 -> x0, matrix products: 19.4 us -> none  [the longest x3 6.37 us: local(): jnp.dot(columns, piece, preferred_element_type=jnp.float32)]
    ppermute x4 -> x0, starting transfers between devices: 17.3 us -> none  [the longest x2 11.7 us: from_behind(): return lax.ppermute(block, axis, route)]
    scatter-add x2 -> x0, local copies, waits for them, and re-layouts: 14.1 us -> none  [the longest x1 7.89 us: local(): inner = inner.at[:, :HALO].add(from_prev)]
    slice x2 -> x0, local copies, waits for them, and re-layouts: 6.32 us -> none  [the longest x1 3.96 us: forward_block(): key_h = near[0].reshape(block, SLOTS, heads, HEAD_DIM)]
  transfers between devices with their start and end apart: 7 -> 0, of which waited for: 4 -> 0; matrix products, arithmetic and copies ran while one was open for 4% -> 0% of each run, Pallas kernels for 0% -> 0%
where the time goes in v1:
time: 101 us
  Pallas kernels  94.5 us (94%)
  local copies, waits for them, and re-layouts  5.7 us (6%)
    pallas_call x1, Pallas kernels, local(): pl.pallas_call(body, out_shape=(jax.ShapeDtypeStruct((ROWS, V // MEMBERS)...  94.5 us
    unnamed x20, local copies, waits for them, and re-layouts  5.7 us

profile of v1, /device:TPU:1, one launch (start us, length us, event | category | flops | bytes accessed | tf_op | source)
XLA Modules:
  0.0 100.9 jit_solution(663783333743450396)
XLA Ops:
  0.6 0.0 copy-start.7
  0.6 0.0 copy-start.2
  0.7 0.8 copy.11.neighbours
  1.5 0.0 copy-done.7
  1.5 0.0 copy-start.3
  1.5 0.0 copy-start.4
  1.5 0.0 copy-start.6
  1.5 0.1 copy.12.slot_mask
  1.6 0.0 copy-done.2
  1.6 0.6 copy-done.3
  2.2 0.0 copy-done.4
  2.3 0.0 copy-done.6
  2.3 0.0 copy-start
  2.3 0.9 copy-done
  3.2 0.0 copy-start.1
  3.2 0.9 copy-done.1
  4.2 0.0 copy-start.5
  4.2 0.8 copy-done.5
  4.9 94.5 %shard_map.104 = (f32[128,16]{1,0:T(8,128)S(1)}, f32[128,1024]{1,0:T(8,128)S(1)}) custom-call(bf16[128,1024]{1,0:T(8,128)(2,1)S(1)} %bitcast.4, f32[1,1024]{1,0:T(1,128)S(1)} %bitcast.5, bf16[16,1024]{1,0:T(8,128)(2,1)S(1)} %copy-done.3, bf16[16,1024]{1,0:T(8,128)(2,1)S(1)} %copy-done.4, bf16[16,1024]{1,0:T(8,128)(2,1)S(1)} %copy-done.5, ...), custom_call_target="tpu_custom_call" | custom-call | tf_op jit(solution)/shard_map/pallas_call | solution.py:395
  99.4 0.7 copy.13
  100.1 0.8 copy.15
Async XLA Ops:
  0.6 0.8 copy-start.7
  0.6 1.0 copy-start.2
  1.5 0.8 copy-start.3
  1.5 0.8 copy-start.4
  1.5 0.8 copy-start.6
  2.3 1.0 copy-start
  3.2 0.9 copy-start.1
  4.2 0.8 copy-start.5

commit v2 on v1

--- a/solution.py
+++ b/solution.py
@@ -24,6 +24,8 @@
 CHIPS = Y * Z_LO
 MESH = pl.DeviceIdType.MESH
 COPIES = 160
+NEXT_TO = [dict(dc=1), dict(dy=1), dict(dy=-1), dict(dy=2), dict(dz=1), dict(dz=-1), dict(dx=1), dict(dx=-1), dict(dx=2)]
+TELL = [[dict(dz=1), dict(dz=-1)], [dict(dz=2), dict(dz=-2)], [dict(dz=4), dict(dz=-4)], [dict(dy=1), dict(dy=-1)]]
 
 F32 = jnp.float32
 BF16 = jnp.bfloat16
@@ -86,7 +88,7 @@
             copy.wait_send()
 
 
-def gather_weights(here, net, w_refs, W, local_sem):
+def gather_weights(here, net, w_refs, W, local_sem, between):
     y, z, c = here.y, here.z % Z_LO, here.core
     mine, other = pl.multiple_of(c * HALF, HALF), pl.multiple_of((1 - c) * HALF, HALF)
     own_rows = pl.ds(pl.multiple_of(c * 16, 16), 16)
@@ -119,6 +121,7 @@
     along_y = [forward(y, z, first, dy=d) for d in (1, -1, 2)]
     second_up, second_down = forward(y, z, second, dz=1), forward(y, z, second, dz=-1)
     pending = [(z, forward(y, z, second, dy=1), forward(y, z, second, dy=-1))]
+    between[0]()
     for copy in along_y:
         copy.wait_recv()
     first_up, first_down = forward(every, z, first, dz=1), forward(every, z, first, dz=-1)
@@ -162,35 +165,37 @@
         for item in pending:
             spread(*item)
         pending = arrived
+        between[step]()
     for item in pending:
         spread(*item)
+    between[last + 1]()
     for zs, copy in relayed:
         copy.wait_recv()
         pass_on(second, far, zs)
+    between[last + 2]()
     for copy in across:
         copy.wait_recv()
 
 
 def body(
-    latent, gain, w_query, w_key, w_value, w_read, target, neighbours, slot_mask,
+    latent, gain_in, w_query, w_key, w_value, w_read_in, target_in, neighbours, slot_mask,
     crps_out, grad_out,
+    gain, w_read, target, slots,
     W, near, normed, inverse, counts, queries, keys, values, probs, mixed,
     part, part_in, field, pull, down, dquery, dkey, dvalue, halo_out, halo_in, back, back_in,
-    send_sem, recv_sem, local_sem,
+    send_sem, recv_sem, local_sem, input_sem, ready,
 ):
     here = Place()
     net = Net(send_sem, recv_sem)
     core = here.core
-    peers = [
-        here.at(dc=1),
-        here.at(dy=1), here.at(dy=-1), here.at(dy=2),
-        here.at(dz=1), here.at(dz=-1), here.at(dz=8),
-        here.at(dx=1), here.at(dx=-1), here.at(dx=2),
-        here.chip(1, core), here.chip(-1, core), here.chip(2 * core - 1, 1 - core),
-    ]
+    inputs = [(gain_in, gain), (w_read_in, w_read), (target_in, target), (neighbours, slots.at[0]), (slot_mask, slots.at[1])]
+    inputs = [pltpu.make_async_copy(src, dst, input_sem.at[i]) for i, (src, dst) in enumerate(inputs)]
+    peers = [here.at(**step) for step in NEXT_TO]
     barrier = pltpu.get_barrier_semaphore()
     for peer in peers:
         pl.semaphore_signal(barrier, inc=1, device_id=peer, device_id_type=MESH)
+    for copy in inputs:
+        copy.start()
     pl.semaphore_wait(barrier, len(peers))
 
     own = pl.ds(pl.multiple_of(HALO + core * ROWS, 64), ROWS)
@@ -198,39 +203,76 @@
     edge_there = pl.ds(pl.multiple_of((1 - core) * (HALO + PAIR), 64), HALO)
     edge_here = pl.ds(pl.multiple_of(core * (HALO + PAIR), 64), HALO)
     own_copy = pltpu.make_async_copy(latent, near.at[own], local_sem.at[3])
-    own_copy.start()
-    pair_copy = net.send(latent, near.at[own], here.at(dc=1))
-    edge_copy = net.send(latent.at[edge], near.at[edge_there], here.chip(2 * core - 1, 1 - core))
-
-    first = here.node * ROWS - HALO
-    total = 2 * CHIPS * ROWS
-    spot = neighbours[...] - first
-    spot = jnp.where(spot < 0, spot + total, spot)
-    spot = jnp.where(spot >= total, spot - total, spot)
-    used = (slot_mask[...] > 0).astype(F32)
-    window = lax.broadcasted_iota(jnp.int32, (ROWS, WINDOW), 1)
-    number = jnp.zeros((ROWS, WINDOW), F32)
-    for j in range(SLOTS):
-        number += jnp.where(spot[:, j : j + 1] == window, used[:, j : j + 1], 0.0)
-    counts[core] = number.astype(BF16)
-    count_copy = net.send(counts.at[core], counts.at[core], here.at(dc=1))
-
-    gather_weights(here, net, (w_query, w_key, w_value), W, local_sem)
-
-    edge_copy.wait_recv()
-    hand_on = net.send(near.at[edge_here], near.at[edge_here], here.at(dc=1))
-    own_copy.wait()
-    pair_copy.wait_recv()
-    hand_on.wait_recv()
-    count_copy.wait_recv()
-
-    @pl.loop(0, NEAR // 64)
-    def _(i):
-        rows = pl.ds(pl.multiple_of(i * 64, 64), 64)
-        wide = near[rows, :].astype(F32)
-        scale = lax.rsqrt(jnp.mean(wide * wide, axis=-1, keepdims=True) + EPSILON)
-        inverse[rows, :] = jnp.broadcast_to(scale, (64, 128))
-        normed[rows, :] = (wide * scale * gain[...]).astype(BF16)
+    copies = {}
+
+    def tell(step):
+        for to in TELL[step]:
+            pl.semaphore_signal(ready.at[step], inc=1, device_id=here.at(**to), device_id_type=MESH)
+
+    def hear(step):
+        pl.semaphore_wait(ready.at[step], len(TELL[step]))
+
+    def normalize(start, count):
+        @pl.loop(0, count // 64)
+        def _(i):
+            rows = pl.ds(pl.multiple_of(start + i * 64, 64), 64)
+            wide = near[rows, :].astype(F32)
+            scale = lax.rsqrt(jnp.mean(wide * wide, axis=-1, keepdims=True) + EPSILON)
+            inverse[rows, :] = jnp.broadcast_to(scale, (64, 128))
+            normed[rows, :] = (wide * scale * gain[...]).astype(BF16)
+
+    def count_slots():
+        for copy in inputs:
+            copy.wait()
+        first = here.node * ROWS - HALO
+        total = 2 * CHIPS * ROWS
+        spot = slots[0] - first
+        spot = jnp.where(spot < 0, spot + total, spot)
+        spot = jnp.where(spot >= total, spot - total, spot)
+        spot = jnp.where(slots[1] > 0, spot, -1).astype(F32).T
+        window = lax.broadcasted_iota(jnp.int32, (ROWS, WINDOW), 1).astype(F32)
+        number = jnp.zeros((ROWS, WINDOW), F32)
+        for j in range(SLOTS):
+            number += jnp.where(spot[:, j : j + 1] == window, 1.0, 0.0)
+        counts[core] = number.astype(BF16)
+        copies["count"] = net.send(counts.at[core], counts.at[core], here.at(dc=1))
+
+    def between_0():
+        own_copy.start()
+        copies["pair"] = net.send(latent, near.at[own], here.at(dc=1))
+        tell(0)
+        count_slots()
+        hear(0)
+        tell(1)
+
+    def between_1():
+        hear(1)
+        tell(2)
+        own_copy.wait()
+        normalize(HALO + core * ROWS, ROWS)
+
+    def between_2():
+        hear(2)
+        tell(3)
+        copies["pair"].wait_recv()
+        normalize(HALO + (1 - core) * ROWS, ROWS)
+
+    def between_3():
+        hear(3)
+        copies["edge"] = net.send(latent.at[edge], near.at[edge_there], here.chip(2 * core - 1, 1 - core))
+
+    def between_5():
+        copies["edge"].wait_recv()
+        copies["hand_on"] = net.send(near.at[edge_here], near.at[edge_here], here.at(dc=1))
+        normalize(core * (HALO + PAIR), HALO)
+
+    def between_6():
+        copies["hand_on"].wait_recv()
+        normalize((1 - core) * (HALO + PAIR), HALO)
+        copies["count"].wait_recv()
+
+    between = [between_0, between_1, between_2, between_3, lambda: None, between_5, between_6]
+    gather_weights(here, net, (w_query, w_key, w_value), W, local_sem, between)
 
     inner = pl.ds(HALO, PAIR)
 
@@ -345,21 +387,6 @@
         piece = W[0, j].reshape(256, HALF)
         back[:, cols] = dot_nt(dquery[...], piece)
 
-    to_prev.wait_recv()
-    to_next.wait_recv()
-    for grad, k in ((dkey, 0), (dvalue, 1)):
-        grad[pl.ds(PAIR, HALO), :] += halo_in[0, k].astype(F32)
-        grad[pl.ds(HALO, HALO), :] += halo_in[1, k].astype(F32)
-
-    @pl.loop(0, D // 256)
-    def _(j):
-        cols = pl.ds(pl.multiple_of(j * 256, 256), 256)
-        back[:, cols] += dot_nt(dkey[inner, :].astype(BF16), W[1, j].reshape(256, HALF)) + dot_nt(
-            dvalue[inner, :].astype(BF16), W[2, j].reshape(256, HALF)
-        )
-
-    back_copy = net.send(back.at[other_rows], back_in, here.at(dc=1))
-
     def abs_of(gap):
         return jnp.sqrt(gap * gap + soft)
 
@@ -371,15 +398,30 @@
             spread += 2.0 * abs_of(field[m] - field[k])
     crps = miss / MEMBERS - spread / (2.0 * MEMBERS * (MEMBERS - 1))
     share = V // MEMBERS
-    crps_out[...] = pltpu.roll(crps, (V - me * share) % V, 1)[:, :share]
+    crps_out[...] = pltpu.roll(crps, (V - me * share) % V, 1).T[:share, :]
+
+    to_prev.wait_recv()
+    to_next.wait_recv()
+    for grad, k in ((dkey, 0), (dvalue, 1)):
+        grad[pl.ds(PAIR, HALO), :] += halo_in[0, k].astype(F32)
+        grad[pl.ds(HALO, HALO), :] += halo_in[1, k].astype(F32)
+
+    @pl.loop(0, D // 256)
+    def _(j):
+        cols = pl.ds(pl.multiple_of(j * 256, 256), 256)
+        back[:, cols] += dot_nt(dkey[inner, :].astype(BF16), W[1, j].reshape(256, HALF)) + dot_nt(
+            dvalue[inner, :].astype(BF16), W[2, j].reshape(256, HALF)
+        )
+
+    back_copy = net.send(back.at[other_rows], back_in, here.at(dc=1))
 
     back_copy.wait_recv()
 
     @pl.loop(0, ROWS // 32)
     def _(i):
         rows = pl.ds(pl.multiple_of(i * 32, 32), 32)
-        wide = latent[rows, :].astype(F32)
         here_rows = pl.ds(pl.multiple_of(HALO + core * ROWS + i * 32, 32), 32)
+        wide = near[here_rows, :].astype(F32)
         factor = inverse[here_rows, 0:1]
         pair_rows = pl.ds(pl.multiple_of(core * ROWS + i * 32, 32), 32)
         scaled = (back[pair_rows, :] + back_in[rows, :]) * gain[...]
@@ -391,13 +433,17 @@
 
 
 def local(latent, gain, w_query, w_key, w_value, w_read, target, neighbours, slot_mask):
-    vmem = pl.BlockSpec(memory_space=pltpu.VMEM)
+    vmem, hbm = pl.BlockSpec(memory_space=pltpu.VMEM), pl.BlockSpec(memory_space=pltpu.HBM)
     crps, grad = pl.pallas_call(
         body,
-        out_shape=(jax.ShapeDtypeStruct((ROWS, V // MEMBERS), F32), jax.ShapeDtypeStruct((ROWS, D), F32)),
-        in_specs=[vmem] * 9,
+        out_shape=(jax.ShapeDtypeStruct((V // MEMBERS, ROWS), F32), jax.ShapeDtypeStruct((ROWS, D), F32)),
+        in_specs=[hbm] * 9,
         out_specs=(vmem, vmem),
         scratch_shapes=[
+            pltpu.VMEM((1, D), F32),
+            pltpu.VMEM((D, V), BF16),
+            pltpu.VMEM((ROWS, V), F32),
+            pltpu.VMEM((2, SLOTS, ROWS), jnp.int32),
             pltpu.VMEM((3, Y, Z_LO, 32, HALF), BF16),
             pltpu.VMEM((NEAR, D), BF16),
             pltpu.VMEM((NEAR, D), BF16),
@@ -423,12 +469,14 @@
             pltpu.SemaphoreType.DMA((COPIES,)),
             pltpu.SemaphoreType.DMA((COPIES,)),
             pltpu.SemaphoreType.DMA((4,)),
+            pltpu.SemaphoreType.DMA((5,)),
+            pltpu.SemaphoreType.REGULAR((len(TELL),)),
         ],
         compiler_params=pltpu.CompilerParams(
-            collective_id=0, has_side_effects=True, vmem_limit_bytes=40 * 1024 * 1024
+            collective_id=0, has_side_effects=True, vmem_limit_bytes=63 * 1024 * 1024
         ),
-    )(latent[0], gain[None], w_query, w_key, w_value, w_read, target, neighbours, slot_mask)
-    return crps, grad[None]
+    )(latent[0], gain[None], w_query, w_key, w_value, w_read, target, neighbours.T, slot_mask.T)
+    return crps.T, grad[None]
 
 
 def solution(mesh):

time: 101 us -> 96 us (0.950)
  Pallas kernels: 94.5 us -> 91.9 us
  local copies, waits for them, and re-layouts: 5.7 us -> 3.18 us
    pallas_call x1, Pallas kernels: 94.5 us -> 91.9 us  [local(): pl.pallas_call(body, out_shape=(jax.ShapeDtypeStruct((V // MEMBERS, ROWS)...]
    unnamed x20 -> x2, local copies, waits for them, and re-layouts: 5.7 us -> 3.18 us
where the time goes in v2:
time: 96 us; the launch traced here: 95.7 us
  Pallas kernels  91.9 us (96%)
  local copies, waits for them, and re-layouts  3.18 us (3%)
    pallas_call x1, Pallas kernels, local(): pl.pallas_call(body, out_shape=(jax.ShapeDtypeStruct((V // MEMBERS, ROWS)...  91.9 us
    unnamed x2, local copies, waits for them, and re-layouts  3.18 us

profile of v2, /device:TPU:1, one launch (start us, length us, event | category | flops | bytes accessed | tf_op | source)
XLA Modules:
  0.0 95.7 jit_solution(17707151476486575506)
XLA Ops:
  0.6 91.9 %shard_map.104 = (f32[16,128]{1,0:T(8,128)}, f32[128,1024]{1,0:T(8,128)}) custom-call(bf16[128,1024]{1,0:T(8,128)(2,1)} %bitcast.7, f32[1,1024]{1,0:T(1,128)} %bitcast.9, bf16[16,1024]{1,0:T(8,128)(2,1)} %w_query.1, bf16[16,1024]{1,0:T(8,128)(2,1)} %w_key.1, bf16[16,1024]{1,0:T(8,128)(2,1)} %w_value.1, bf16[1024,128]{1,0:T(8,128)(2,1)} %w_read_in.1, ...), custom_call_target="tpu_custom_call" | custom-call | tf_op jit(solution)/shard_map/pallas_call | solution.py:437
  92.5 1.3 %copy.13 = f32[128,16]{0,1:T(8,128)} copy(f32[128,16]{0,1:T(8,128)} %bitcast.8) | data formatting | bytes 16384
  93.8 1.9 %copy.14 = f32[1,128,1024]{2,1,0:T(8,128)} copy(f32[1,128,1024]{2,1,0:T(8,128)} %bitcast.6) | data formatting | bytes 1048576

commit v3 on v2

--- a/solution.py
+++ b/solution.py
@@ -118,26 +118,31 @@
 
     every = slice(None)
     below, above, far = (y + 3) % Y, (y + 1) % Y, (y + 2) % Y
+    def spread(zs):
+        return (zs, [forward(y, zs, second, dy=d) for d in (1, -1, 2)])
+
+    def settle(zs, copies):
+        for copy in copies:
+            copy.wait_recv()
+        for ys in (below, above, far) if zs is z else (below, above, far, y):
+            pass_on(second, ys, zs)
+
+    def forward_first(piece, zs, **step):
+        k, ys = piece
+        part = W.at[here.x % 2 + k, ys, zs, first]
+        return net.send(part, part, here.at(**step))
+
+    second_up, second_down = forward(y, z, second, dz=1), forward(y, z, second, dz=-1)
     along_y = [forward(y, z, first, dy=d) for d in (1, -1, 2)]
-    second_up, second_down = forward(y, z, second, dz=1), forward(y, z, second, dz=-1)
-    pending = [(z, forward(y, z, second, dy=1), forward(y, z, second, dy=-1))]
+    pending = [spread(z)]
     between[0]()
     for copy in along_y:
         copy.wait_recv()
-    first_up, first_down = forward(every, z, first, dz=1), forward(every, z, first, dz=-1)
+    pieces = [(k, pl.ds(2 * j, 2)) for j in range(2) for k in range(2)]
+    up = [forward_first(piece, z, dz=1) for piece in pieces]
+    down = [forward_first(piece, z, dz=-1) for piece in pieces]
     for ys in (below, above, far):
         pass_on(first, ys, z)
-    relayed = []
-
-    def spread(zs, from_below, from_above):
-        from_below.wait_recv()
-        from_above.wait_recv()
-        if len(relayed) % 2 == 0:
-            relayed.append((zs, forward(below, zs, second, dy=1)))
-        else:
-            relayed.append((zs, forward(above, zs, second, dy=-1)))
-        for ys in (below, above) if zs is z else (below, above, y):
-            pass_on(second, ys, zs)
 
     last = Z_LO // 2
     for step in range(1, last + 1):
@@ -147,31 +152,34 @@
             second_up.wait_recv()
             if step < last - 1:
                 second_up = forward(y, before, second, dz=1)
-            arrived.append((before, forward(y, before, second, dy=1), forward(y, before, second, dy=-1)))
         second_down.wait_recv()
         if step < last:
             second_down = forward(y, after, second, dz=-1)
-        arrived.append((after, forward(y, after, second, dy=1), forward(y, after, second, dy=-1)))
-        first_up.wait_recv()
-        first_down.wait_recv()
-        if step < last - 1:
-            first_up, first_down = forward(every, before, first, dz=1), forward(every, after, first, dz=-1)
-        elif step == last - 1:
-            first_up = forward(pl.ds(0, 2), before, first, dz=1)
-            first_down = forward(pl.ds(2, 2), after, first, dz=-1)
+            arrived.append(spread(before))
+        arrived.append(spread(after))
         if step < last:
+            next_up, next_down = [], []
+            for i, piece in enumerate(pieces):
+                up[i].wait_recv()
+                if step < last - 1 or i < 2:
+                    next_up.append(forward_first(piece, before, dz=1))
+                down[i].wait_recv()
+                if step < last - 1 or i >= 2:
+                    next_down.append(forward_first(piece, after, dz=-1))
+            up, down = next_up, next_down
             pass_on(first, every, before)
-        pass_on(first, every, after)
+            pass_on(first, every, after)
+        else:
+            for copy in up + down:
+                copy.wait_recv()
+            pass_on(first, every, after)
         for item in pending:
-            spread(*item)
+            settle(*item)
         pending = arrived
         between[step]()
     for item in pending:
-        spread(*item)
+        settle(*item)
     between[last + 1]()
-    for zs, copy in relayed:
-        copy.wait_recv()
-        pass_on(second, far, zs)
     between[last + 2]()
     for copy in across:
         copy.wait_recv()
@@ -292,94 +300,121 @@
         return jnp.concatenate([piece * low_b, piece * high_b], axis=0)
 
     def one_piece(both):
-        return jnp.where(lanes < HEAD_DIM, both[:ROWS], both[ROWS:])
-
-    def places(i):
-        block, group = i // GROUPS, i % GROUPS
-        rows = pl.ds(pl.multiple_of(block * ROWS, ROWS), ROWS)
-        around = pl.ds(pl.multiple_of(block * ROWS, ROWS), WINDOW)
-        return block, rows, around, pl.ds(pl.multiple_of(group * 128, 128), 128)
-
-    def count_of(block):
-        one = counts[block].astype(F32)
+        return jnp.where(lanes < HEAD_DIM, both[:HALO], both[HALO:])
+
+    def start_of(half, block):
+        return block * ROWS + HALO * ((half + block) % 2)
+
+    def places(half, block, group):
+        rows = pl.ds(start_of(half, block), HALO)
+        around = pl.ds(block * ROWS, WINDOW)
+        return rows, around, pl.ds(pl.multiple_of(group * 128, 128), 128)
+
+    def count_of(half, block):
+        one = counts[block, pl.ds(HALO * ((half + block) % 2), HALO), :].astype(F32)
         return jnp.concatenate([one, one], axis=0)
 
-    @pl.loop(0, 2 * GROUPS)
-    def _(i):
-        block, rows, around, cols = places(i)
-        number = count_of(block)
-        scores = dot_nt(two_heads(queries[rows, cols]), keys[around, cols])
-        weight = jnp.where(number > 0, jnp.exp(scores * scale), 0.0)
-        prob = weight / jnp.sum(number * weight, axis=-1, keepdims=True)
-        probs[i] = prob
-        share = (prob.astype(BF16).astype(F32) * number).astype(BF16)
-        mixed[rows, cols] = one_piece(dot(share, values[around, cols]))
-
     mine = pl.ds(pl.multiple_of(core * HALF, HALF), HALF)
-    updated = (near[inner, mine].astype(F32) + mixed[...]).astype(BF16)
-    reader = w_read[mine, :]
-    part[...] = dot(updated, reader)
-    mine_rows = pl.ds(pl.multiple_of(core * ROWS, ROWS), ROWS)
-    other_rows = pl.ds(pl.multiple_of((1 - core) * ROWS, ROWS), ROWS)
-    part_copy = net.send(part.at[other_rows], part_in, here.at(dc=1))
-    part_copy.wait_recv()
     me = here.member
-    field[me] = part[mine_rows, :] + part_in[...]
-
     partner = (me + X) % MEMBERS
-    along = [net.send(field.at[me], field.at[me], here.at(dx=d)) for d in (1, -1, 2)]
-    pieces = [pl.ds(k * 32, 32) for k in range(4)]
-    over = [net.send(field.at[me, rows], field.at[me, rows], here.at(dz=8)) for rows in pieces]
-    for copy, rows in zip(over, pieces):
-        copy.wait_recv()
-        piece = field.at[partner, rows]
-        along += [net.send(piece, piece, here.at(dx=d)) for d in (1, -1, 2)]
-    for copy in along:
-        copy.wait_recv()
+    fields = [{}, {}]
+
+    def own_rows(half, offset=0, count=HALO):
+        return pl.ds(pl.multiple_of(HALO * ((half + core) % 2) + offset, 32), count)
+
+    def attend(half):
+        @pl.loop(0, GROUPS)
+        def _(group):
+            for block in range(2):
+                rows, around, cols = places(half, block, group)
+                number = count_of(half, block)
+                scores = dot_nt(two_heads(queries[rows, cols]), keys[around, cols])
+                weight = jnp.where(number > 0, jnp.exp(scores * scale), 0.0)
+                prob = weight / jnp.sum(number * weight, axis=-1, keepdims=True)
+                probs[half, block, group] = prob
+                share = (prob.astype(BF16).astype(F32) * number).astype(BF16)
+                mixed[rows, cols] = one_piece(dot(share, values[around, cols]))
+
+    def read_out(half):
+        for block in range(2):
+            rows = pl.ds(start_of(half, block), HALO)
+            wide = near[pl.ds(HALO + start_of(half, block), HALO), mine].astype(F32)
+            part[rows, :] = dot((wide + mixed[rows, :]).astype(BF16), w_read[mine, :])
+        theirs = pl.ds(pl.multiple_of((1 - core) * ROWS + HALO * ((half + 1 - core) % 2), 64), HALO)
+        ours = pl.ds(pl.multiple_of(core * ROWS + HALO * ((half + core) % 2), 64), HALO)
+        net.send(part.at[theirs], part_in.at[half], here.at(dc=1)).wait_recv()
+        field[me, own_rows(half), :] = part[ours, :] + part_in[half]
+        pieces = [field.at[me, own_rows(half, 32 * k, 32)] for k in range(2)]
+        fields[half]["over"] = [net.send(piece, piece, here.at(dz=8)) for piece in pieces]
+        whole = field.at[me, own_rows(half)]
+        fields[half]["along"] = [net.send(whole, whole, here.at(dx=d)) for d in (1, -1, 2)]
+
+    def relay(half):
+        for k, copy in enumerate(fields[half]["over"]):
+            copy.wait_recv()
+            piece = field.at[partner, own_rows(half, 32 * k, 32)]
+            fields[half]["along"] += [net.send(piece, piece, here.at(dx=d)) for d in (1, -1, 2)]
 
     soft = SOFTNESS * SOFTNESS
-    here_field = field[me]
 
     def sign_of(gap):
         return gap * lax.rsqrt(gap * gap + soft)
 
-    returned = sign_of(here_field - field[0])
-    for m in range(1, MEMBERS):
-        returned += sign_of(here_field - field[m])
-    pulled = sign_of(here_field - target[...]) - returned / (MEMBERS - 1)
-    pull[core] = pulled.astype(BF16)
-    pull_copy = net.send(pull.at[core], pull.at[core], here.at(dc=1))
-    pull_copy.wait_recv()
-    down[...] = dot_nt(pull[...].reshape(PAIR, V), reader).astype(BF16)
-
-    dkey[...] = jnp.zeros_like(dkey)
-    dvalue[...] = jnp.zeros_like(dvalue)
-
-    def backward(i, carry):
-        block, rows, around, cols = places(i)
-        number = count_of(block)
-        prob = probs[i]
-        given = two_heads(down[rows, cols])
-        asked = two_heads(queries[rows, cols])
-        share = (prob.astype(BF16).astype(F32) * number).astype(BF16)
-        dprob = dot_nt(given, values[around, cols])
-        level = jnp.sum(number * prob * dprob, axis=-1, keepdims=True)
-        dscaled = (prob * (dprob - level) * scale).astype(BF16)
-        dscaled = (dscaled.astype(F32) * number).astype(BF16)
-        dquery[rows, cols] = one_piece(dot(dscaled, keys[around, cols])).astype(BF16)
-        dkey[around, cols] += dot_tn(dscaled, asked)
-        dvalue[around, cols] += dot_tn(share, given)
-        return carry
+    def pull_back(half):
+        for copy in fields[half]["along"]:
+            copy.wait_recv()
+        rows = own_rows(half)
+        here_field = field[me, rows, :]
+        returned = sign_of(here_field - field[0, rows, :])
+        for m in range(1, MEMBERS):
+            returned += sign_of(here_field - field[m, rows, :])
+        pulled = sign_of(here_field - target[rows, :]) - returned / (MEMBERS - 1)
+        pull[core, rows, :] = pulled.astype(BF16)
+        piece = pull.at[core, rows]
+        net.send(piece, piece, here.at(dc=1)).wait_recv()
+        for block in range(2):
+            there = pull[block, pl.ds(HALO * ((half + block) % 2), HALO), :]
+            down[pl.ds(start_of(half, block), HALO), :] = dot_nt(there, w_read[mine, :]).astype(BF16)
+
+    def backward(half):
+        @pl.loop(0, GROUPS)
+        def _(group):
+            for block in range(2):
+                rows, around, cols = places(half, block, group)
+                number = count_of(half, block)
+                prob = probs[half, block, group]
+                given = two_heads(down[rows, cols])
+                asked = two_heads(queries[rows, cols])
+                share = (prob.astype(BF16).astype(F32) * number).astype(BF16)
+                dprob = dot_nt(given, values[around, cols])
+                level = jnp.sum(number * prob * dprob, axis=-1, keepdims=True)
+                dscaled = (prob * (dprob - level) * scale).astype(BF16)
+                dscaled = (dscaled.astype(F32) * number).astype(BF16)
+                dquery[rows, cols] = one_piece(dot(dscaled, keys[around, cols])).astype(BF16)
+                dkey[around, cols] += dot_tn(dscaled, asked)
+                dvalue[around, cols] += dot_tn(share, given)
 
     def send_halo(side, rows, step):
         halo_out[side, 0] = dkey[rows, :].astype(BF16)
         halo_out[side, 1] = dvalue[rows, :].astype(BF16)
         return net.send(halo_out.at[side], halo_in.at[side], here.chip(step, core))
 
-    lax.fori_loop(0, GROUPS, backward, 0)
+    for half in range(2):
+        attend(half)
+        read_out(half)
+    dkey[...] = jnp.zeros_like(dkey)
+    dvalue[...] = jnp.zeros_like(dvalue)
+    relay(0)
+    relay(1)
+    pull_back(0)
+    backward(0)
     to_prev = send_halo(0, pl.ds(0, HALO), -1)
-    lax.fori_loop(GROUPS, 2 * GROUPS, backward, 0)
     to_next = send_halo(1, pl.ds(HALO + PAIR, HALO), 1)
+    pull_back(1)
+    backward(1)
+
+    mine_rows = pl.ds(pl.multiple_of(core * ROWS, ROWS), ROWS)
+    other_rows = pl.ds(pl.multiple_of((1 - core) * ROWS, ROWS), ROWS)
 
     @pl.loop(0, D // 256)
     def _(j):
@@ -452,10 +487,10 @@
             pltpu.VMEM((PAIR, HALF), BF16),
             pltpu.VMEM((NEAR, HALF), BF16),
             pltpu.VMEM((NEAR, HALF), BF16),
-            pltpu.VMEM((2 * GROUPS, 2 * ROWS, WINDOW), F32),
+            pltpu.VMEM((2, 2, GROUPS, 2 * HALO, WINDOW), F32),
             pltpu.VMEM((PAIR, HALF), F32),
             pltpu.VMEM((PAIR, V), F32),
-            pltpu.VMEM((ROWS, V), F32),
+            pltpu.VMEM((2, HALO, V), F32),
             pltpu.VMEM((MEMBERS, ROWS, V), F32),
             pltpu.VMEM((2, ROWS, V), BF16),
             pltpu.VMEM((PAIR, HALF), BF16),

time: 96 us -> 87.5 us (0.911)
  Pallas kernels: 91.9 us -> 83.5 us
    pallas_call x1, Pallas kernels: 91.9 us -> 83.5 us  [local(): pl.pallas_call(body, out_shape=(jax.ShapeDtypeStruct((V // MEMBERS, ROWS)...]
where the time goes in v3:
time: 87.5 us; the launch traced here: 87.3 us
  Pallas kernels  83.5 us (95%)
  local copies, waits for them, and re-layouts  3.18 us (4%)
    pallas_call x1, Pallas kernels, local(): pl.pallas_call(body, out_shape=(jax.ShapeDtypeStruct((V // MEMBERS, ROWS)...  83.5 us
    unnamed x2, local copies, waits for them, and re-layouts  3.18 us

profile of v3, /device:TPU:1, one launch (start us, length us, event | category | flops | bytes accessed | tf_op | source)
XLA Modules:
  0.0 87.3 jit_solution(16660416474172250757)
XLA Ops:
  0.6 83.5 %shard_map.104 = (f32[16,128]{1,0:T(8,128)}, f32[128,1024]{1,0:T(8,128)}) custom-call(bf16[128,1024]{1,0:T(8,128)(2,1)} %bitcast.7, f32[1,1024]{1,0:T(1,128)} %bitcast.9, bf16[16,1024]{1,0:T(8,128)(2,1)} %w_query.1, bf16[16,1024]{1,0:T(8,128)(2,1)} %w_key.1, bf16[16,1024]{1,0:T(8,128)(2,1)} %w_value.1, bf16[1024,128]{1,0:T(8,128)(2,1)} %w_read_in.1, ...), custom_call_target="tpu_custom_call" | custom-call | tf_op jit(solution)/shard_map/pallas_call | solution.py:472
  84.1 1.3 %copy.13 = f32[128,16]{0,1:T(8,128)} copy(f32[128,16]{0,1:T(8,128)} %bitcast.8) | data formatting | bytes 16384
  85.4 1.9 %copy.14 = f32[1,128,1024]{2,1,0:T(8,128)} copy(f32[1,128,1024]{2,1,0:T(8,128)} %bitcast.6) | data formatting | bytes 1048576

commit v4 on v3

--- a/solution.py
+++ b/solution.py
@@ -180,7 +180,6 @@
     for item in pending:
         settle(*item)
     between[last + 1]()
-    between[last + 2]()
     for copy in across:
         copy.wait_recv()
 
@@ -252,34 +251,32 @@
         count_slots()
         hear(0)
         tell(1)
-
-    def between_1():
         hear(1)
         tell(2)
+
+    def between_1():
+        hear(2)
+        tell(3)
+
+    def between_2():
+        hear(3)
+        copies["edge"] = net.send(latent.at[edge], near.at[edge_there], here.chip(2 * core - 1, 1 - core))
+
+    def between_4():
         own_copy.wait()
         normalize(HALO + core * ROWS, ROWS)
-
-    def between_2():
-        hear(2)
-        tell(3)
-        copies["pair"].wait_recv()
-        normalize(HALO + (1 - core) * ROWS, ROWS)
-
-    def between_3():
-        hear(3)
-        copies["edge"] = net.send(latent.at[edge], near.at[edge_there], here.chip(2 * core - 1, 1 - core))
 
     def between_5():
         copies["edge"].wait_recv()
         copies["hand_on"] = net.send(near.at[edge_here], near.at[edge_here], here.at(dc=1))
+        copies["pair"].wait_recv()
+        normalize(HALO + (1 - core) * ROWS, ROWS)
         normalize(core * (HALO + PAIR), HALO)
-
-    def between_6():
         copies["hand_on"].wait_recv()
         normalize((1 - core) * (HALO + PAIR), HALO)
         copies["count"].wait_recv()
 
-    between = [between_0, between_1, between_2, between_3, lambda: None, between_5, between_6]
+    between = [between_0, between_1, between_2, lambda: None, between_4, between_5]
     gather_weights(here, net, (w_query, w_key, w_value), W, local_sem, between)
 
     inner = pl.ds(HALO, PAIR)
@@ -376,9 +373,8 @@
             there = pull[block, pl.ds(HALO * ((half + block) % 2), HALO), :]
             down[pl.ds(start_of(half, block), HALO), :] = dot_nt(there, w_read[mine, :]).astype(BF16)
 
-    def backward(half):
-        @pl.loop(0, GROUPS)
-        def _(group):
+    def backward(half, after=None):
+        def one_group(group):
             for block in range(2):
                 rows, around, cols = places(half, block, group)
                 number = count_of(half, block)
@@ -394,10 +390,22 @@
                 dkey[around, cols] += dot_tn(dscaled, asked)
                 dvalue[around, cols] += dot_tn(share, given)
 
-    def send_halo(side, rows, step):
-        halo_out[side, 0] = dkey[rows, :].astype(BF16)
-        halo_out[side, 1] = dvalue[rows, :].astype(BF16)
-        return net.send(halo_out.at[side], halo_in.at[side], here.chip(step, core))
+        if after is None:
+            pl.loop(0, GROUPS)(one_group)
+        else:
+            for group in range(GROUPS):
+                one_group(group)
+                after(group)
+
+    halos = []
+
+    def send_halos(group):
+        cols = pl.ds(group * 128, 128)
+        for side, rows, step in ((0, pl.ds(0, HALO), -1), (1, pl.ds(HALO + PAIR, HALO), 1)):
+            halo_out[side, 0, :, cols] = dkey[rows, cols].astype(BF16)
+            halo_out[side, 1, :, cols] = dvalue[rows, cols].astype(BF16)
+            piece = (side, slice(None), slice(None), cols)
+            halos.append(net.send(halo_out.at[piece], halo_in.at[piece], here.chip(step, core)))
 
     for half in range(2):
         attend(half)
@@ -407,9 +415,7 @@
     relay(0)
     relay(1)
     pull_back(0)
-    backward(0)
-    to_prev = send_halo(0, pl.ds(0, HALO), -1)
-    to_next = send_halo(1, pl.ds(HALO + PAIR, HALO), 1)
+    backward(0, send_halos)
     pull_back(1)
     backward(1)
 
@@ -435,22 +441,21 @@
     share = V // MEMBERS
     crps_out[...] = pltpu.roll(crps, (V - me * share) % V, 1).T[:share, :]
 
-    to_prev.wait_recv()
-    to_next.wait_recv()
+    for copy in halos:
+        copy.wait_recv()
     for grad, k in ((dkey, 0), (dvalue, 1)):
         grad[pl.ds(PAIR, HALO), :] += halo_in[0, k].astype(F32)
         grad[pl.ds(HALO, HALO), :] += halo_in[1, k].astype(F32)
 
-    @pl.loop(0, D // 256)
-    def _(j):
-        cols = pl.ds(pl.multiple_of(j * 256, 256), 256)
+    back_copies = []
+    for j in range(D // 256):
+        cols = pl.ds(j * 256, 256)
         back[:, cols] += dot_nt(dkey[inner, :].astype(BF16), W[1, j].reshape(256, HALF)) + dot_nt(
             dvalue[inner, :].astype(BF16), W[2, j].reshape(256, HALF)
         )
-
-    back_copy = net.send(back.at[other_rows], back_in, here.at(dc=1))
-
-    back_copy.wait_recv()
+        back_copies.append(net.send(back.at[other_rows, cols], back_in.at[:, cols], here.at(dc=1)))
+    for copy in back_copies:
+        copy.wait_recv()
 
     @pl.loop(0, ROWS // 32)
     def _(i):

time: 87.5 us -> 82.6 us (0.944)
  Pallas kernels: 83.5 us -> 78.5 us
    pallas_call x1, Pallas kernels: 83.5 us -> 78.5 us  [local(): pl.pallas_call(body, out_shape=(jax.ShapeDtypeStruct((V // MEMBERS, ROWS)...]
where the time goes in v4:
time: 82.6 us; the launch traced here: 82.3 us
  Pallas kernels  78.5 us (95%)
  local copies, waits for them, and re-layouts  3.18 us (4%)
    pallas_call x1, Pallas kernels, local(): pl.pallas_call(body, out_shape=(jax.ShapeDtypeStruct((V // MEMBERS, ROWS)...  78.5 us
    unnamed x2, local copies, waits for them, and re-layouts  3.18 us

profile of v4, /device:TPU:1, one launch (start us, length us, event | category | flops | bytes accessed | tf_op | source)
XLA Modules:
  0.0 82.3 jit_solution(17051619568026331730)
XLA Ops:
  0.6 78.5 %shard_map.104 = (f32[16,128]{1,0:T(8,128)}, f32[128,1024]{1,0:T(8,128)}) custom-call(bf16[128,1024]{1,0:T(8,128)(2,1)} %bitcast.7, f32[1,1024]{1,0:T(1,128)} %bitcast.9, bf16[16,1024]{1,0:T(8,128)(2,1)} %w_query.1, bf16[16,1024]{1,0:T(8,128)(2,1)} %w_key.1, bf16[16,1024]{1,0:T(8,128)(2,1)} %w_value.1, bf16[1024,128]{1,0:T(8,128)(2,1)} %w_read_in.1, ...), custom_call_target="tpu_custom_call" | custom-call | tf_op jit(solution)/shard_map/pallas_call | solution.py:477
  79.1 1.3 %copy.13 = f32[128,16]{0,1:T(8,128)} copy(f32[128,16]{0,1:T(8,128)} %bitcast.8) | data formatting | bytes 16384
  80.4 1.9 %copy.14 = f32[1,128,1024]{2,1,0:T(8,128)} copy(f32[1,128,1024]{2,1,0:T(8,128)} %bitcast.6) | data formatting | bytes 1048576

commit v5 on v4

--- a/solution.py
+++ b/solution.py
@@ -320,8 +320,7 @@
         return pl.ds(pl.multiple_of(HALO * ((half + core) % 2) + offset, 32), count)
 
     def attend(half):
-        @pl.loop(0, GROUPS)
-        def _(group):
+        for group in range(GROUPS):
             for block in range(2):
                 rows, around, cols = places(half, block, group)
                 number = count_of(half, block)
@@ -391,7 +390,8 @@
                 dvalue[around, cols] += dot_tn(share, given)
 
         if after is None:
-            pl.loop(0, GROUPS)(one_group)
+            for group in range(GROUPS):
+                one_group(group)
         else:
             for group in range(GROUPS):
                 one_group(group)

time: 82.6 us -> 80.9 us (0.979)
  Pallas kernels: 78.5 us -> 76.9 us
    pallas_call x1, Pallas kernels: 78.5 us -> 76.9 us  [local(): pl.pallas_call(body, out_shape=(jax.ShapeDtypeStruct((V // MEMBERS, ROWS)...]
where the time goes in v5:
time: 80.9 us; the launch traced here: 80.7 us
  Pallas kernels  76.9 us (95%)
  local copies, waits for them, and re-layouts  3.18 us (4%)
    pallas_call x1, Pallas kernels, local(): pl.pallas_call(body, out_shape=(jax.ShapeDtypeStruct((V // MEMBERS, ROWS)...  76.9 us
    unnamed x2, local copies, waits for them, and re-layouts  3.18 us

profile of v5, /device:TPU:1, one launch (start us, length us, event | category | flops | bytes accessed | tf_op | source)
XLA Modules:
  0.0 80.7 jit_solution(4068997492427180116)
XLA Ops:
  0.6 76.9 %shard_map.104 = (f32[16,128]{1,0:T(8,128)}, f32[128,1024]{1,0:T(8,128)}) custom-call(bf16[128,1024]{1,0:T(8,128)(2,1)} %bitcast.7, f32[1,1024]{1,0:T(1,128)} %bitcast.9, bf16[16,1024]{1,0:T(8,128)(2,1)} %w_query.1, bf16[16,1024]{1,0:T(8,128)(2,1)} %w_key.1, bf16[16,1024]{1,0:T(8,128)(2,1)} %w_value.1, bf16[1024,128]{1,0:T(8,128)(2,1)} %w_read_in.1, ...), custom_call_target="tpu_custom_call" | custom-call | tf_op jit(solution)/shard_map/pallas_call | solution.py:477
  77.5 1.3 %copy.13 = f32[128,16]{0,1:T(8,128)} copy(f32[128,16]{0,1:T(8,128)} %bitcast.8) | data formatting | bytes 16384
  78.8 1.9 %copy.14 = f32[1,128,1024]{2,1,0:T(8,128)} copy(f32[1,128,1024]{2,1,0:T(8,128)} %bitcast.6) | data formatting | bytes 1048576
